TPU v7x, 512 devices: a whole 4x4x16 slice. The times are simulated.
512 devices in a mesh: ma: 64 (over x, z), freq: 8 (over y, core).
Axes of the slice: x: 4, y: 4, z: 16, core: 2. Of those that a mesh axis runs over, the one named last changes fastest.
Arguments:
- visibility: bfloat16 [8, 64, 512, 512], P('freq', 'ma'), may hold values from -6 to 6
- noise_weight: float32 [8, 64, 512], P('freq', 'ma'), may hold values from 0.25 to 2
- transfer: bfloat16 [8, 64, 4, 2, 128, 512], P('freq', 'ma'), may hold values from -0.25 to 0.25
- legendre: bfloat16 [64, 4, 128, 128], P('ma'), may hold values from -0.25 to 0.25
- tile_count: int32 [64], replicated, may hold values from 1 to 4, as said below
Outputs:
- cycle_modes: bfloat16 [128, 64, 512], P('ma', None, 'freq')
Inputs may be any that keep to these rules, and one draw needn't show every extreme that they name: Only the first tile_count[j] slots of transfer and legendre for m-mode j are used.
All inputs are finite; a program needn't handle non-finite values.
Results may differ from a plain program's by a relative error of at most 0.019.
Values may be sent and summed in bfloat16 or wider, within the bound.
No kernel may reach another device: no remote copies, remote signals or barrier semaphores. Data moves between devices by JAX's collectives and lax.ppermute only.
A program may use at most 64 MiB of HBM per device.

v0:
```python
import jax
import jax.numpy as jnp
from jax import lax
from jax.sharding import PartitionSpec as P


def coeff_tile(beam_tile, weighted):
    real_rows = jnp.dot(beam_tile[0], weighted, preferred_element_type=jnp.float32)
    imag_rows = jnp.dot(beam_tile[1], weighted, preferred_element_type=jnp.float32)
    half_sets = weighted.shape[1] // 2
    real_coeff = real_rows[:, :half_sets] + imag_rows[:, half_sets:]
    imag_coeff = real_rows[:, half_sets:] - imag_rows[:, :half_sets]
    return jnp.concatenate([real_coeff, imag_coeff], axis=1).astype(jnp.bfloat16)


def tile_sum(first_tile, stop_tile, beam_set, cycle_set, weighted):

    def add_tile(slot_index, running):
        coeffs = coeff_tile(beam_set[slot_index], weighted)
        return running + jnp.dot(cycle_set[slot_index], coeffs, preferred_element_type=jnp.float32)

    empty_sum = jnp.zeros((cycle_set.shape[1], weighted.shape[1]), jnp.float32)
    return lax.fori_loop(first_tile, stop_tile, add_tile, empty_sum)


def local(visibility, noise_weight, transfer, legendre, tile_count):
    weighted = (noise_weight[0, 0][:, None] * visibility[0, 0].astype(jnp.float32)).astype(
        jnp.bfloat16
    )
    beam_set = transfer[0, 0]
    cycle_set = legendre[0]
    position = lax.axis_index("ma")
    own_count = tile_count[position]
    modes_sum = tile_sum(0, own_count, beam_set, cycle_set, weighted)
    modes = modes_sum[:, None, :]
    by_cycles = lax.all_to_all(
        modes.astype(jnp.bfloat16), "ma", split_axis=0, concat_axis=1, tiled=True
    ).astype(modes.dtype)
    band_total = lax.psum_scatter(
        by_cycles.astype(jnp.bfloat16), "freq", scatter_dimension=2, tiled=True
    ).astype(jnp.float32)
    return (band_total / lax.axis_size("freq")).astype(jnp.bfloat16)


def solution(mesh):
    return jax.shard_map(
        local,
        mesh=mesh,
        in_specs=(
            P("freq", "ma", None, None),
            P("freq", "ma", None),
            P("freq", "ma", None, None, None, None),
            P("ma", None, None, None),
            P(),
        ),
        out_specs=P("ma", None, "freq"),
        check_vma=False,
    )
```

profile of v0, /device:TPU:1, one launch (start us, length us, event | category | flops | bytes accessed | tf_op | source)
XLA Modules:
  0.0 128.2 jit_solution(12804172658768382069)
XLA Ops:
  6.5 1.3 %dynamic_slice.9 = s32[1]{0:T(128)} dynamic-slice(s32[64]{0:T(128)} %param.11, s32[]{:T(128)S(6)} %select_n.7), dynamic_slice_sizes={1} | dynamic-slice | bytes 12 | tf_op jit(solution)/shard_map/dynamic_slice | solution.py:33
  7.9 1.2 fusion.13
  9.1 16.6 %while.10 = (s32[]{:T(128)}, f32[128,512]{1,0:T(8,128)S(1)}, s32[]{:T(128)}, bf16[4,128,128]{2,1,0:T(8,128)(2,1)}, bf16[4,2,128,512]{3,2,1,0:T(8,128)(2,1)}, /*i...) while((s32[]{:T(128)}, f32[128,512]{1,0:T(8,128)S(1)}, s32[]{:T(128)}, ...), condition=%wide.region_1.0_spmd, body=%wide.region_0.0_spmd.sunk | while | flops 151453696 | bytes 3178667 | solution.py:23
  9.8 1.1 fusion.27
  10.9 1.1 fusion.28
  12.1 0.9 convolution_add_fusion.2
  13.8 1.1 fusion.27
  14.9 1.1 fusion.28
  16.1 0.9 convolution_add_fusion.2
  17.8 1.1 fusion.27
  18.9 1.1 fusion.28
  20.1 0.9 convolution_add_fusion.2
  21.8 1.1 fusion.27
  22.9 1.1 fusion.28
  24.1 0.9 convolution_add_fusion.2
  26.3 0.7 reduce.1
  27.0 30.4 %all_to_all.18 = bf16[64,2,512]{2,1,0:T(2,128)(2,1)S(1)} all-to-all(bf16[64,2,512]{2,1,0:T(2,128)(2,1)S(1)} %reshape.12), channel_id=1, replica_groups=mesh['ma'=64,'freq'=8] {'ma'}, dimensions={0} | all-to-all | bytes 262144 | tf_op jit(solution)/shard_map/all_to_all | solution.py:36
  57.5 0.8 reduce
  58.4 13.7 %copy.12 = bf16[2,64,512]{0,1,2:T(8,128)(2,1)} copy(bf16[2,64,512]{2,0,1:T(2,128)(2,1)S(1)} %bitcast.39) | data formatting | bytes 262144
  72.1 13.7 %reshape.9 = bf16[512,128]{1,0:T(8,128)(2,1)} reshape(bf16[512,64,2]{2,1,0:T(8,128)(2,1)} %bitcast.36) | data formatting | bytes 262144
  85.8 30.7 %reduce-scatter.4.cloned.1.call-done = bf16[64,128]{1,0:T(8,128)(2,1)} async-done(((bf16[512,128]{1,0:T(8,128)(2,1)}), bf16[64,128]{1,0:T(8,128)(2,1)}) %reduce-scatter.4.cloned.1.call-update) | async-done | bytes 16400
  116.5 3.0 %reshape.10 = bf16[64,64,2]{2,1,0:T(8,128)(2,1)S(1)} reshape(bf16[64,128]{1,0:T(8,128)(2,1)} %reduce-scatter.4.cloned.1.call-done) | data formatting | bytes 32768
  119.5 1.3 copy.11
  120.7 0.6 multiply_convert_fusion
  (12 shorter events, 0.9 us)
Async XLA Ops:
  6.5 110.0 %reduce-scatter.4.cloned.1.call-start = ((), (), s32[]{:S(2)}) async-start(), calls=%async_computation.2 | async-start | bytes 147456
Sparse Core Ops, SparseCore 0:
  85.9 30.5 reduce-scatter.3
where the time goes:
time: 130 us; the launch traced here: 128 us
  local copies, waits for them, and re-layouts  33.7 us (26%)
  waiting for transfers between devices  30.7 us (24%)
  blocking collectives  30.4 us (23%)
  between operations  13.5 us (10%)
  matrix products  12.9 us (10%)
  loops' own time  3.63 us (3%)
  other arithmetic  3.43 us (3%)
    unnamed x2, waiting for transfers between devices  30.7 us
    unnamed x5, local copies, waits for them, and re-layouts  30.5 us
    all_to_all x1, blocking collectives, local(): lax.all_to_all(modes.astype(jnp.bfloat16), 'ma', split_axis=0, concat_axi...  30.4 us
    dot_general x4, matrix products, coeff_tile(): jnp.dot(beam_tile[0], weighted, preferred_element_type=jnp.float32)  4.54 us
    dot_general x4, matrix products, coeff_tile(): jnp.dot(beam_tile[1], weighted, preferred_element_type=jnp.float32)  4.54 us
    dot_general x4, matrix products, add_tile(): jnp.dot(cycle_set[slot_index], coeffs, preferred_element_type=jnp.float32)  3.79 us
    another operation x1, loops' own time, tile_sum(): return lax.fori_loop(first_tile, stop_tile, add_tile, empty_sum)  3.63 us
  transfers between devices with their start and end apart: 1, of which 1 were waited for; matrix products, arithmetic and copies ran while one was open for 0% of the time, Pallas kernels for 0%

commit v1 on v0

v1 whole, which is shorter than its diff:
```python
import jax
import jax.numpy as jnp
from jax import lax
from jax.experimental import pallas as pl
from jax.experimental.pallas import tpu as pltpu
from jax.sharding import PartitionSpec as P

NVIS = 512
LT = 128
SLOTS = 4
SETS = 512
RINGS = 128
BANDS = 8
CYCLES = 64


def modes_kernel(
    count_ref, vis_hbm, noise_hbm, beam_hbm, cycle_hbm, out_ref,
    vis, noise, beam, cycle, weighted, coeff, acc, sem,
):
    copies = [
        pltpu.make_async_copy(noise_hbm.at[0], noise, sem.at[0]),
        pltpu.make_async_copy(vis_hbm.at[0, 0], vis, sem.at[1]),
    ]
    beam_copies = [
        pltpu.make_async_copy(beam_hbm.at[0, 0, s], beam.at[s], sem.at[2 + s])
        for s in range(SLOTS)
    ]
    cycle_copy = pltpu.make_async_copy(cycle_hbm.at[0], cycle, sem.at[2 + SLOTS])
    for copy in copies + beam_copies + [cycle_copy]:
        copy.start()
    own_count = count_ref[lax.axis_index("ma")]

    copies[0].wait()
    column = jnp.broadcast_to(noise[...], (LT, NVIS)).T
    copies[1].wait()
    for k in range(SETS // 128):
        lanes = pl.ds(128 * k, 128)
        weighted[:, lanes] = (column * vis[:, lanes].astype(jnp.float32)).astype(jnp.bfloat16)

    half = SETS // 2
    for s in range(SLOTS):
        beam_copies[s].wait()
        tile = beam[s].reshape(2 * LT, NVIS)
        rows = jnp.dot(tile, weighted[...], preferred_element_type=jnp.float32)
        real, imag = rows[:LT], rows[LT:]
        keep = s < own_count
        coeff[pl.ds(s * LT, LT), :half] = jnp.where(
            keep, real[:, :half] + imag[:, half:], 0.0
        ).astype(jnp.bfloat16)
        coeff[pl.ds(s * LT, LT), half:] = jnp.where(
            keep, real[:, half:] - imag[:, :half], 0.0
        ).astype(jnp.bfloat16)

    cycle_copy.wait()
    synth = jnp.concatenate([cycle[s] for s in range(SLOTS)], axis=1)
    total = jnp.dot(synth, coeff[...], preferred_element_type=jnp.float32)

    low = lax.broadcasted_iota(jnp.int32, (CYCLES, 128), 1) < 64
    for k in range(SETS // 128):
        acc[k] = total[:, 128 * k : 128 * (k + 1)]
        even = acc[k, pl.ds(0, CYCLES, stride=2), :]
        odd = acc[k, pl.ds(1, CYCLES, stride=2), :]
        out_ref[2 * k] = jnp.where(low, even, pltpu.roll(odd, 64, 1)).astype(jnp.bfloat16)
        out_ref[2 * k + 1] = jnp.where(low, pltpu.roll(even, 64, 1), odd).astype(jnp.bfloat16)


def sum_kernel(band_ref, out_ref):
    total = band_ref[0].astype(jnp.float32)
    for f in range(1, BANDS):
        total += band_ref[f].astype(jnp.float32)
    out_ref[...] = total * (1.0 / BANDS)


def split_kernel(cycle_ref, out_ref):
    rows = cycle_ref[...].astype(jnp.bfloat16)
    out_ref[0] = rows[:, :64]
    out_ref[1] = rows[:, 64:]


def local(visibility, noise_weight, transfer, legendre, tile_count):
    bands = pl.pallas_call(
        modes_kernel,
        out_shape=jax.ShapeDtypeStruct((BANDS, CYCLES, 128), jnp.bfloat16),
        in_specs=[pl.BlockSpec(memory_space=pltpu.SMEM)]
        + [pl.BlockSpec(memory_space=pl.ANY)] * 4,
        out_specs=pl.BlockSpec(memory_space=pltpu.VMEM),
        scratch_shapes=[
            pltpu.VMEM((NVIS, SETS), jnp.bfloat16),
            pltpu.VMEM((1, NVIS), jnp.float32),
            pltpu.VMEM((SLOTS, 2, LT, NVIS), jnp.bfloat16),
            pltpu.VMEM((SLOTS, RINGS, LT), jnp.bfloat16),
            pltpu.VMEM((NVIS, SETS), jnp.bfloat16),
            pltpu.VMEM((SLOTS * LT, SETS), jnp.bfloat16),
            pltpu.VMEM((SETS // 128, RINGS, 128), jnp.float32),
            pltpu.SemaphoreType.DMA((3 + SLOTS,)),
        ],
        compiler_params=pltpu.CompilerParams(vmem_limit_bytes=60 * 1024 * 1024),
    )(tile_count, visibility, noise_weight, transfer, legendre)
    by_band = lax.all_to_all(bands, "freq", 0, 0, tiled=True)
    in_vmem = pl.BlockSpec(memory_space=pltpu.VMEM)
    band_sum = pl.pallas_call(
        sum_kernel,
        out_shape=jax.ShapeDtypeStruct((CYCLES, 128), jnp.float32),
        in_specs=[in_vmem],
        out_specs=in_vmem,
    )(by_band)
    by_cycle = lax.all_to_all(band_sum.reshape(CYCLES, 1, 128), "ma", 0, 0, tiled=True)
    return pl.pallas_call(
        split_kernel,
        out_shape=jax.ShapeDtypeStruct((2, CYCLES, 64), jnp.bfloat16),
        in_specs=[in_vmem],
        out_specs=in_vmem,
    )(by_cycle.reshape(CYCLES, 128))


def solution(mesh):
    return jax.shard_map(
        local,
        mesh=mesh,
        in_specs=(
            P("freq", "ma", None, None),
            P("freq", "ma", None),
            P("freq", "ma", None, None, None, None),
            P("ma", None, None, None),
            P(),
        ),
        out_specs=P("ma", None, "freq"),
        check_vma=False,
    )
```

time: 130 us -> 50.8 us (0.39); the launches traced: 128 us -> 50.5 us
  local copies, waits for them, and re-layouts: 33.7 us -> 0 us
  waiting for transfers between devices: 30.7 us -> 0 us
  between operations: 13.5 us -> 0.01 us
  matrix products: 12.9 us -> 0 us
  blocking collectives: 30.4 us -> 42.9 us
  Pallas kernels: 0 us -> 7.54 us
  loops' own time: 3.63 us -> 0 us
  other arithmetic: 3.43 us -> 0 us
    unnamed x2 -> x0, waiting for transfers between devices: 30.7 us -> none
    unnamed x5 -> x0, local copies, waits for them, and re-layouts: 30.5 us -> none
    dot_general x12 -> x0, matrix products: 12.9 us -> none  [the longest x4 4.54 us: coeff_tile(): jnp.dot(beam_tile[0], weighted, preferred_element_type=jnp.float32)]
    all_to_all x1 -> x2, blocking collectives: 30.4 us -> 42.9 us  [the longest x1 26.8 us: local(): lax.all_to_all(band_sum.reshape(CYCLES, 1, 128), 'ma', 0, 0, tiled=True)]
    pallas_call x0 -> x3, Pallas kernels: none -> 7.54 us  [the longest x1 4.55 us: local(): pl.pallas_call(modes_kernel, out_shape=jax.ShapeDtypeStruct((BANDS, CYCLE...]
    another operation x1 -> x0, loops' own time: 3.63 us -> none  [tile_sum(): return lax.fori_loop(first_tile, stop_tile, add_tile, empty_sum)]
    convert_element_type x4 -> x0, other arithmetic: 2.53 us -> none  [the longest x1 1.21 us: local(): (noise_weight[0, 0][:, None] * visibility[0, 0].astype(jnp.float32)).asty...]
    dynamic_slice x1 -> x0, local copies, waits for them, and re-layouts: 1.32 us -> none  [local(): own_count = tile_count[position]]
  transfers between devices with their start and end apart: 1 -> 0, of which waited for: 1 -> 0; matrix products, arithmetic and copies ran while one was open for 0% -> 0% of each run, Pallas kernels for 0% -> 0%
where the time goes in v1:
time: 50.8 us; the launch traced here: 50.5 us
  blocking collectives  42.9 us (84%)
  Pallas kernels  7.54 us (15%)
    all_to_all x1, blocking collectives, local(): lax.all_to_all(band_sum.reshape(CYCLES, 1, 128), 'ma', 0, 0, tiled=True)  26.8 us
    all_to_all x1, blocking collectives, local(): by_band = lax.all_to_all(bands, 'freq', 0, 0, tiled=True)  16.1 us
    pallas_call x1, Pallas kernels, local(): pl.pallas_call(modes_kernel, out_shape=jax.ShapeDtypeStruct((BANDS, CYCLE...  4.55 us
    pallas_call x1, Pallas kernels, local(): pl.pallas_call(sum_kernel, out_shape=jax.ShapeDtypeStruct((CYCLES, 128),...  1.54 us
    pallas_call x1, Pallas kernels, local(): pl.pallas_call(split_kernel, out_shape=jax.ShapeDtypeStruct((2, CYCLES, 6...  1.45 us

profile of v1, /device:TPU:1, one launch (start us, length us, event | category | flops | bytes accessed | tf_op | source)
XLA Modules:
  0.0 50.5 jit_solution(15786006011736188320)
XLA Ops:
  0.0 4.5 %shard_map.55 = bf16[8,64,128]{2,1,0:T(8,128)(2,1)} custom-call(s32[64]{0:T(128)} %count_ref.1, bf16[1,1,512,512]{3,2,1,0:T(8,128)(2,1)} %vis_hbm.1, f32[1,1,512]{2,1,0:T(1,128)} %noise_hbm.1, bf16[1,1,4,2,128,512]{5,4,3,2,1,0:T(8,128)(2,1)} %beam_hbm.1, bf16[1,4,128,128]{3,2,1,0:T(8,128)(2,1)} %cycle_hbm.1), custom_call_target="tpu_custom_call" | custom-call | tf_op jit(solution)/shard_map/pallas_call | solution.py:82
  4.6 16.1 %all_to_all.10.band_ref = bf16[8,64,128]{2,1,0:T(8,128)(2,1)} all-to-all(bf16[8,64,128]{2,1,0:T(8,128)(2,1)} %shard_map.55), channel_id=1, replica_groups=mesh['ma'=64,'freq'=8] {'freq'}, dimensions={0} | all-to-all | bytes 262144 | tf_op jit(solution)/shard_map/all_to_all | solution.py:100
  20.7 1.5 %shard_map.56 = f32[64,128]{1,0:T(8,128)} custom-call(bf16[8,64,128]{2,1,0:T(8,128)(2,1)} %all_to_all.10.band_ref), custom_call_target="tpu_custom_call" | custom-call | tf_op jit(solution)/shard_map/pallas_call | solution.py:102
  22.2 26.8 %all_to_all.11 = f32[64,1,128]{2,1,0:T(1,128)} all-to-all(f32[64,1,128]{2,1,0:T(1,128)} %bitcast.4), channel_id=1, replica_groups=mesh['ma'=64,'freq'=8] {'ma'}, dimensions={0} | all-to-all | bytes 65536 | tf_op jit(solution)/shard_map/all_to_all | solution.py:108
  49.0 1.4 %shard_map.57 = bf16[2,64,64]{2,1,0:T(8,128)(2,1)} custom-call(f32[64,128]{1,0:T(8,128)} %bitcast.5), custom_call_target="tpu_custom_call" | custom-call | tf_op jit(solution)/shard_map/pallas_call | solution.py:109

commit v2 on v1

v2 whole, which is shorter than its diff:
```python
import jax
import jax.numpy as jnp
from jax import lax
from jax.experimental import pallas as pl
from jax.experimental.pallas import tpu as pltpu
from jax.sharding import PartitionSpec as P

NVIS = 512
LT = 128
SLOTS = 4
SETS = 512
RINGS = 128
BANDS = 8
CYCLES = 64


def modes_kernel(
    count_hbm, vis_hbm, noise_hbm, beam_hbm, cycle_hbm, out_ref,
    vis, noise, beam, cycle, weighted, coeff, acc, count, sem,
):
    copies = [
        pltpu.make_async_copy(noise_hbm.at[0], noise, sem.at[0]),
        pltpu.make_async_copy(vis_hbm.at[0, 0], vis, sem.at[1]),
    ]
    beam_copies = [
        pltpu.make_async_copy(beam_hbm.at[0, 0, s], beam.at[s], sem.at[2 + s])
        for s in range(SLOTS)
    ]
    cycle_copy = pltpu.make_async_copy(cycle_hbm.at[0], cycle, sem.at[2 + SLOTS])
    count_copy = pltpu.make_async_copy(count_hbm, count, sem.at[3 + SLOTS])
    for copy in [count_copy] + copies + beam_copies + [cycle_copy]:
        copy.start()

    copies[0].wait()
    column = jnp.broadcast_to(noise[...], (LT, NVIS)).T
    copies[1].wait()
    for k in range(SETS // 128):
        lanes = pl.ds(128 * k, 128)
        weighted[:, lanes] = (column * vis[:, lanes].astype(jnp.float32)).astype(jnp.bfloat16)

    count_copy.wait()
    own_count = count[lax.axis_index("ma")]
    half = SETS // 2
    for s in range(SLOTS):
        beam_copies[s].wait()
        real = jnp.dot(beam[s, 0], weighted[...], preferred_element_type=jnp.float32)
        imag = jnp.dot(beam[s, 1], weighted[...], preferred_element_type=jnp.float32)
        keep = s < own_count
        coeff[pl.ds(s * LT, LT), :half] = jnp.where(
            keep, real[:, :half] + imag[:, half:], 0.0
        ).astype(jnp.bfloat16)
        coeff[pl.ds(s * LT, LT), half:] = jnp.where(
            keep, real[:, half:] - imag[:, :half], 0.0
        ).astype(jnp.bfloat16)

    cycle_copy.wait()
    synth = jnp.concatenate([cycle[s] for s in range(SLOTS)], axis=1)
    total = jnp.dot(synth, coeff[...], preferred_element_type=jnp.float32)

    low = lax.broadcasted_iota(jnp.int32, (CYCLES, 128), 1) < 64
    for k in range(SETS // 128):
        acc[k] = total[:, 128 * k : 128 * (k + 1)]
        even = acc[k, pl.ds(0, CYCLES, stride=2), :]
        odd = acc[k, pl.ds(1, CYCLES, stride=2), :]
        out_ref[2 * k] = jnp.where(low, even, pltpu.roll(odd, 64, 1)).astype(jnp.bfloat16)
        out_ref[2 * k + 1] = jnp.where(low, pltpu.roll(even, 64, 1), odd).astype(jnp.bfloat16)


def local(visibility, noise_weight, transfer, legendre, tile_count):
    bands = pl.pallas_call(
        modes_kernel,
        out_shape=pltpu.VMEM((BANDS, CYCLES, 128), jnp.bfloat16),
        in_specs=[pl.BlockSpec(memory_space=pl.ANY)] * 5,
        out_specs=pl.BlockSpec(memory_space=pltpu.VMEM),
        scratch_shapes=[
            pltpu.VMEM((NVIS, SETS), jnp.bfloat16),
            pltpu.VMEM((1, NVIS), jnp.float32),
            pltpu.VMEM((SLOTS, 2, LT, NVIS), jnp.bfloat16),
            pltpu.VMEM((SLOTS, RINGS, LT), jnp.bfloat16),
            pltpu.VMEM((NVIS, SETS), jnp.bfloat16),
            pltpu.VMEM((SLOTS * LT, SETS), jnp.bfloat16),
            pltpu.VMEM((SETS // 128, RINGS, 128), jnp.float32),
            pltpu.SMEM((CYCLES,), jnp.int32),
            pltpu.SemaphoreType.DMA((4 + SLOTS,)),
        ],
        compiler_params=pltpu.CompilerParams(vmem_limit_bytes=56 * 1024 * 1024),
    )(tile_count, visibility, noise_weight, transfer, legendre)
    by_band = lax.all_to_all(bands, "freq", 0, 0, tiled=True)
    band_sum = jnp.sum(by_band.astype(jnp.float32), axis=0) * (1.0 / BANDS)
    by_cycle = lax.all_to_all(
        band_sum.reshape(CYCLES, 1, 128), "ma", 0, 0, tiled=True
    ).reshape(CYCLES, 128)
    return jnp.stack([by_cycle[:, :64], by_cycle[:, 64:]]).astype(jnp.bfloat16)


def solution(mesh):
    return jax.shard_map(
        local,
        mesh=mesh,
        in_specs=(
            P("freq", "ma", None, None),
            P("freq", "ma", None),
            P("freq", "ma", None, None, None, None),
            P("ma", None, None, None),
            P(),
        ),
        out_specs=P("ma", None, "freq"),
        check_vma=False,
    )
```

time: 50.8 us -> 46.4 us (0.913)
  Pallas kernels: 7.54 us -> 3.07 us
  other arithmetic: 0 us -> 0.66 us
    pallas_call x3 -> x1, Pallas kernels: 7.54 us -> 3.07 us  [local(): pl.pallas_call(modes_kernel, out_shape=pltpu.VMEM((BANDS, CYCLES, 128), j...]
    all_to_all x1, blocking collectives: 16.1 us -> 14.5 us  [local(): by_band = lax.all_to_all(bands, 'freq', 0, 0, tiled=True)]
    all_to_all x1, blocking collectives: 26.8 us -> 27.9 us  [local(): lax.all_to_all(band_sum.reshape(CYCLES, 1, 128), 'ma', 0, 0, tiled=True)]
    another operation x0 -> x2, other arithmetic: none -> 0.63 us  [the longest x1 0.63 us: local(): return jnp.stack([by_cycle[:, :64], by_cycle[:, 64:]]).astype(jnp.bfloat16)]
where the time goes in v2:
time: 46.4 us; the launch traced here: 46.2 us
  blocking collectives  42.4 us (91%)
  Pallas kernels  3.07 us (7%)
  other arithmetic  0.66 us (1%)
    all_to_all x1, blocking collectives, local(): lax.all_to_all(band_sum.reshape(CYCLES, 1, 128), 'ma', 0, 0, tiled=True)  27.9 us
    all_to_all x1, blocking collectives, local(): by_band = lax.all_to_all(bands, 'freq', 0, 0, tiled=True)  14.5 us
    pallas_call x1, Pallas kernels, local(): pl.pallas_call(modes_kernel, out_shape=pltpu.VMEM((BANDS, CYCLES, 128), j...  3.07 us

profile of v2, /device:TPU:1, one launch (start us, length us, event | category | flops | bytes accessed | tf_op | source)
XLA Modules:
  0.0 46.2 jit_solution(2753350336682198541)
XLA Ops:
  0.0 3.1 %shard_map.55 = bf16[8,64,128]{2,1,0:T(8,128)(2,1)S(1)} custom-call(s32[64]{0:T(128)} %count_hbm.1, bf16[1,1,512,512]{3,2,1,0:T(8,128)(2,1)} %vis_hbm.1, f32[1,1,512]{2,1,0:T(1,128)} %noise_hbm.1, bf16[1,1,4,2,128,512]{5,4,3,2,1,0:T(8,128)(2,1)} %beam_hbm.1, bf16[1,4,128,128]{3,2,1,0:T(8,128)(2,1)} %cycle_hbm.1), custom_call_target="tpu_custom_call" | custom-call | tf_op jit(solution)/shard_map/pallas_call | solution.py:70
  3.1 14.5 %all_to_all.10 = bf16[8,64,128]{2,1,0:T(8,128)(2,1)S(1)} all-to-all(bf16[8,64,128]{2,1,0:T(8,128)(2,1)S(1)} %shard_map.55), channel_id=1, replica_groups=mesh['ma'=64,'freq'=8] {'freq'}, dimensions={0} | all-to-all | bytes 262144 | tf_op jit(solution)/shard_map/all_to_all | solution.py:88
  17.6 27.9 %all_to_all.11 = f32[64,1,128]{2,1,0:T(1,128)S(1)} all-to-all(f32[64,1,128]{2,1,0:T(1,128)S(1)} %bitcast.8), channel_id=1, replica_groups=mesh['ma'=64,'freq'=8] {'ma'}, dimensions={0} | all-to-all | bytes 65536 | tf_op jit(solution)/shard_map/all_to_all | solution.py:90
  45.5 0.1 slice_bitcast_fusion.1
  45.6 0.6 %pad_maximum_fusion = bf16[2,64,64]{2,1,0:T(8,128)(2,1)} fusion(bf16[1,64,64]{2,1,0:T(8,128)(2,1)S(1)} %get-tuple-element.6, bf16[1,64,64]{2,1,0:T(8,128)(2,1)S(1)} %get-tuple-element.5), kind=kLoop, calls=%fused_computation.1 | loop fusion | flops 8192 | bytes 32768 | tf_op jit(solution)/shard_map/stack | solution.py:93
  (3 shorter events, 0.0 us)

commit v3 on v2

--- a/solution.py
+++ b/solution.py
@@ -12,6 +12,11 @@
 RINGS = 128
 BANDS = 8
 CYCLES = 64
+
+FIRST_BAND = 5
+FIRST_MODE = 40
+F_ORDER = [(i + FIRST_BAND) % BANDS for i in range(BANDS)]
+M_ORDER = [(i + FIRST_MODE) % CYCLES for i in range(CYCLES)]
 
 
 def modes_kernel(
@@ -60,10 +65,15 @@
     low = lax.broadcasted_iota(jnp.int32, (CYCLES, 128), 1) < 64
     for k in range(SETS // 128):
         acc[k] = total[:, 128 * k : 128 * (k + 1)]
-        even = acc[k, pl.ds(0, CYCLES, stride=2), :]
-        odd = acc[k, pl.ds(1, CYCLES, stride=2), :]
-        out_ref[2 * k] = jnp.where(low, even, pltpu.roll(odd, 64, 1)).astype(jnp.bfloat16)
-        out_ref[2 * k + 1] = jnp.where(low, pltpu.roll(even, 64, 1), odd).astype(jnp.bfloat16)
+        even, odd = (
+            jnp.concatenate([
+                acc[k, pl.ds(2 * FIRST_MODE + p, CYCLES - FIRST_MODE, stride=2), :],
+                acc[k, pl.ds(p, FIRST_MODE, stride=2), :],
+            ])
+            for p in range(2)
+        )
+        out_ref[F_ORDER.index(2 * k)] = jnp.where(low, even, pltpu.roll(odd, 64, 1)).astype(jnp.bfloat16)
+        out_ref[F_ORDER.index(2 * k + 1)] = jnp.where(low, pltpu.roll(even, 64, 1), odd).astype(jnp.bfloat16)
 
 
 def local(visibility, noise_weight, transfer, legendre, tile_count):
@@ -85,11 +95,12 @@
         ],
         compiler_params=pltpu.CompilerParams(vmem_limit_bytes=56 * 1024 * 1024),
     )(tile_count, visibility, noise_weight, transfer, legendre)
-    by_band = lax.all_to_all(bands, "freq", 0, 0, tiled=True)
+    by_band = lax.all_to_all(bands, "freq", 0, 0, tiled=True, axis_index_groups=[F_ORDER])
     band_sum = jnp.sum(by_band.astype(jnp.float32), axis=0) * (1.0 / BANDS)
     by_cycle = lax.all_to_all(
-        band_sum.reshape(CYCLES, 1, 128), "ma", 0, 0, tiled=True
+        band_sum.reshape(CYCLES, 1, 128), "ma", 0, 0, tiled=True, axis_index_groups=[M_ORDER]
     ).reshape(CYCLES, 128)
+    by_cycle = jnp.concatenate([by_cycle[CYCLES - FIRST_MODE :], by_cycle[: CYCLES - FIRST_MODE]])
     return jnp.stack([by_cycle[:, :64], by_cycle[:, 64:]]).astype(jnp.bfloat16)
 
 

time: 46.4 us -> 37.4 us (0.81)
  the two profiles are of different devices: /device:TPU:1 before, /device:TPU:16 now
where the time goes in v3:
time: 37.4 us; the launch traced here: 37.2 us
  blocking collectives  33.4 us (89%)
  Pallas kernels  3.08 us (8%)
  other arithmetic  0.66 us (2%)
    all_to_all x1, blocking collectives, local(): lax.all_to_all(band_sum.reshape(CYCLES, 1, 128), 'ma', 0, 0, tiled=True,...  20.7 us
    all_to_all x1, blocking collectives, local(): lax.all_to_all(bands, 'freq', 0, 0, tiled=True, axis_index_groups=[F_ORDER])  12.6 us
    pallas_call x1, Pallas kernels, local(): pl.pallas_call(modes_kernel, out_shape=pltpu.VMEM((BANDS, CYCLES, 128), j...  3.08 us

profile of v3, /device:TPU:16, one launch (start us, length us, event | category | flops | bytes accessed | tf_op | source)
XLA Modules:
  0.0 37.2 jit_solution(5058492942384752232)
XLA Ops:
  0.0 3.1 %shard_map.55 = bf16[8,64,128]{2,1,0:T(8,128)(2,1)S(1)} custom-call(s32[64]{0:T(128)} %count_hbm.1, bf16[1,1,512,512]{3,2,1,0:T(8,128)(2,1)} %vis_hbm.1, f32[1,1,512]{2,1,0:T(1,128)} %noise_hbm.1, bf16[1,1,4,2,128,512]{5,4,3,2,1,0:T(8,128)(2,1)} %beam_hbm.1, bf16[1,4,128,128]{3,2,1,0:T(8,128)(2,1)} %cycle_hbm.1), custom_call_target="tpu_custom_call" | custom-call | tf_op jit(solution)/shard_map/pallas_call | solution.py:80
  3.1 12.6 %all_to_all.10 = bf16[8,64,128]{2,1,0:T(8,128)(2,1)S(1)} all-to-all(bf16[8,64,128]{2,1,0:T(8,128)(2,1)S(1)} %shard_map.55), channel_id=1, replica_groups={{5,6,7,0,1,2,3,4},{13,14,15,8,9,10,11,12},{21,22,23,16,17,18,19,20},{29..., dimensions={0} | all-to-all | bytes 262144 | tf_op jit(solution)/shard_map/all_to_all | solution.py:98
  15.8 20.7 %all_to_all.11 = f32[64,1,128]{2,1,0:T(1,128)S(1)} all-to-all(f32[64,1,128]{2,1,0:T(1,128)S(1)} %bitcast.7), channel_id=1, replica_groups={{320,328,336,344,352,360,368,376,384,392,400,408,416,424,432,440,448,45..., dimensions={0} | all-to-all | bytes 65536 | tf_op jit(solution)/shard_map/all_to_all | solution.py:100
  36.5 0.1 slice_bitcast_fusion.1
  36.6 0.6 %pad_maximum_fusion = bf16[2,64,64]{2,1,0:T(8,128)(2,1)} fusion(bf16[1,64,64]{2,1,0:T(8,128)(2,1)S(1)} %get-tuple-element.6, bf16[1,64,64]{2,1,0:T(8,128)(2,1)S(1)} %get-tuple-element.5), kind=kLoop, calls=%fused_computation.2 | loop fusion | flops 8192 | bytes 32768 | tf_op jit(solution)/shard_map/stack | solution.py:104
  (5 shorter events, 0.0 us)

commit v4 on v3

v4 whole, which is shorter than its diff:
```python
import jax
import jax.numpy as jnp
from jax import lax
from jax.experimental import pallas as pl
from jax.experimental.pallas import tpu as pltpu
from jax.sharding import PartitionSpec as P

NVIS = 512
LT = 128
SLOTS = 4
SETS = 512
RINGS = 128
BANDS = 8
CYCLES = 64
XS = 4
ZS = 16

FIRST_BAND = 5
FIRST_X = 2
FIRST_Z = 8
F_ORDER = [(i + FIRST_BAND) % BANDS for i in range(BANDS)]
X_ORDER = [(i + FIRST_X) % XS for i in range(XS)]
Z_ORDER = [(i + FIRST_Z) % ZS for i in range(ZS)]
RUNS = [(x * ZS + z, ZS // 2) for x in X_ORDER for z in (FIRST_Z, 0)]
SLAB_GROUPS = [
    [(x * ZS + z) * BANDS + f for x in X_ORDER for f in F_ORDER] for z in range(ZS)
]
LINE_GROUPS = [[x * ZS + z for z in Z_ORDER] for x in range(XS)]


def modes_kernel(
    count_hbm, vis_hbm, noise_hbm, beam_hbm, cycle_hbm, out_ref,
    vis, noise, beam, cycle, weighted, gain, acc, count, sem,
):
    count_copy = pltpu.make_async_copy(count_hbm, count, sem.at[0])
    noise_copy = pltpu.make_async_copy(noise_hbm.at[0], noise, sem.at[1])
    vis_copy = pltpu.make_async_copy(vis_hbm.at[0, 0], vis, sem.at[2])
    cycle_copy = pltpu.make_async_copy(cycle_hbm.at[0], cycle, sem.at[3])
    beam_copy = pltpu.make_async_copy(beam_hbm.at[0, 0], beam, sem.at[4])
    for copy in (count_copy, noise_copy, vis_copy, cycle_copy, beam_copy):
        copy.start()

    noise_copy.wait()
    column = jnp.broadcast_to(noise[...], (LT, NVIS)).T
    vis_copy.wait()
    for k in range(SETS // 128):
        lanes = pl.ds(128 * k, 128)
        weighted[:, lanes] = (column * vis[:, lanes].astype(jnp.float32)).astype(jnp.bfloat16)

    count_copy.wait()
    own_count = count[lax.axis_index("ma")]
    cycle_copy.wait()
    synth = jnp.concatenate(
        [
            jnp.where(s < own_count, cycle[s], jnp.zeros((RINGS, LT), jnp.bfloat16))
            for s in range(SLOTS)
        ],
        axis=1,
    )
    beam_copy.wait()
    for part in range(2):
        tiles = beam[:, part].reshape(SLOTS * LT, NVIS)
        gain[pl.ds(part * RINGS, RINGS)] = jnp.dot(
            synth, tiles, preferred_element_type=jnp.float32
        ).astype(jnp.bfloat16)

    rows = jnp.dot(gain[...], weighted[...], preferred_element_type=jnp.float32)
    real, imag = rows[:RINGS], rows[RINGS:]
    half = SETS // 2
    total = jnp.concatenate(
        [real[:, :half] + imag[:, half:], real[:, half:] - imag[:, :half]], axis=1
    )

    low = lax.broadcasted_iota(jnp.int32, (CYCLES, 128), 1) < 64
    for k in range(SETS // 128):
        acc[k] = total[:, 128 * k : 128 * (k + 1)]
        even, odd = (
            jnp.concatenate([acc[k, pl.ds(2 * d + p, n, stride=2), :] for d, n in RUNS])
            for p in range(2)
        )
        low_band = jnp.where(low, even, pltpu.roll(odd, 64, 1)).astype(jnp.bfloat16)
        high_band = jnp.where(low, pltpu.roll(even, 64, 1), odd).astype(jnp.bfloat16)
        for i in range(XS):
            rows = slice(ZS * i, ZS * (i + 1))
            out_ref[i, F_ORDER.index(2 * k)] = low_band[rows]
            out_ref[i, F_ORDER.index(2 * k + 1)] = high_band[rows]


def local(visibility, noise_weight, transfer, legendre, tile_count):
    bands = pl.pallas_call(
        modes_kernel,
        out_shape=pltpu.VMEM((XS, BANDS, ZS, 128), jnp.bfloat16),
        in_specs=[pl.BlockSpec(memory_space=pl.ANY)] * 5,
        out_specs=pl.BlockSpec(memory_space=pltpu.VMEM),
        scratch_shapes=[
            pltpu.VMEM((NVIS, SETS), jnp.bfloat16),
            pltpu.VMEM((1, NVIS), jnp.float32),
            pltpu.VMEM((SLOTS, 2, LT, NVIS), jnp.bfloat16),
            pltpu.VMEM((SLOTS, RINGS, LT), jnp.bfloat16),
            pltpu.VMEM((NVIS, SETS), jnp.bfloat16),
            pltpu.VMEM((2 * RINGS, NVIS), jnp.bfloat16),
            pltpu.VMEM((SETS // 128, RINGS, 128), jnp.float32),
            pltpu.SMEM((CYCLES,), jnp.int32),
            pltpu.SemaphoreType.DMA((5,)),
        ],
        compiler_params=pltpu.CompilerParams(vmem_limit_bytes=56 * 1024 * 1024),
    )(tile_count, visibility, noise_weight, transfer, legendre)
    by_slab = lax.all_to_all(
        bands.reshape(XS * BANDS, ZS, 128),
        ("ma", "freq"), 0, 0, tiled=True, axis_index_groups=SLAB_GROUPS,
    )
    band_sum = jnp.sum(by_slab.reshape(XS, BANDS, ZS, 128).astype(jnp.float32), axis=1)
    by_line = lax.all_to_all(
        (band_sum * (1.0 / BANDS)).transpose(1, 0, 2),
        "ma", 0, 0, tiled=True, axis_index_groups=LINE_GROUPS,
    )
    modes = by_line.transpose(1, 0, 2)
    modes = jnp.concatenate([modes[:, ZS - FIRST_Z :], modes[:, : ZS - FIRST_Z]], axis=1)
    modes = jnp.concatenate([modes[XS - FIRST_X :], modes[: XS - FIRST_X]]).reshape(CYCLES, 128)
    return jnp.stack([modes[:, :64], modes[:, 64:]]).astype(jnp.bfloat16)


def solution(mesh):
    return jax.shard_map(
        local,
        mesh=mesh,
        in_specs=(
            P("freq", "ma", None, None),
            P("freq", "ma", None),
            P("freq", "ma", None, None, None, None),
            P("ma", None, None, None),
            P(),
        ),
        out_specs=P("ma", None, "freq"),
        check_vma=False,
    )
```

time: 37.4 us -> 35.9 us (0.960)
  the two profiles are of different devices: /device:TPU:16 before, /device:TPU:1 now
where the time goes in v4:
time: 35.9 us; the launch traced here: 35.6 us
  blocking collectives  32.6 us (91%)
  Pallas kernels  2.1 us (6%)
  other arithmetic  0.66 us (2%)
    all_to_all x1, blocking collectives, local(): lax.all_to_all((band_sum * (1.0 / BANDS)).transpose(1, 0, 2), 'ma', 0, 0,...  16.4 us
    all_to_all x1, blocking collectives, local(): lax.all_to_all(bands.reshape(XS * BANDS, ZS, 128), ('ma', 'freq'), 0, 0,...  16.3 us
    pallas_call x1, Pallas kernels, local(): pl.pallas_call(modes_kernel, out_shape=pltpu.VMEM((XS, BANDS, ZS, 128), j...  2.1 us

profile of v4, /device:TPU:1, one launch (start us, length us, event | category | flops | bytes accessed | tf_op | source)
XLA Modules:
  0.0 35.6 jit_solution(10442317228180965351)
XLA Ops:
  0.0 2.1 %shard_map.55 = bf16[4,8,16,128]{3,2,1,0:T(8,128)(2,1)S(1)} custom-call(s32[64]{0:T(128)} %count_hbm.1, bf16[1,1,512,512]{3,2,1,0:T(8,128)(2,1)} %vis_hbm.1, f32[1,1,512]{2,1,0:T(1,128)} %noise_hbm.1, bf16[1,1,4,2,128,512]{5,4,3,2,1,0:T(8,128)(2,1)} %beam_hbm.1, bf16[1,4,128,128]{3,2,1,0:T(8,128)(2,1)} %cycle_hbm.1), custom_call_target="tpu_custom_call" | custom-call | tf_op jit(solution)/shard_map/pallas_call | solution.py:90
  2.1 16.3 %all_to_all.10 = bf16[32,16,128]{2,1,0:T(8,128)(2,1)S(1)} all-to-all(bf16[32,16,128]{2,1,0:T(8,128)(2,1)S(1)} %bitcast.14), channel_id=1, replica_groups={{261,262,263,256,257,258,259,260,389,390,391,384,385,386,387,388,5,6,7,..., dimensions={0} | all-to-all | bytes 262144 | tf_op jit(solution)/shard_map/all_to_all | solution.py:108
  18.4 16.4 %all_to_all.11 = bf16[16,4,128]{2,1,0:T(4,128)(2,1)S(1)} all-to-all(bf16[16,4,128]{2,1,0:T(4,128)(2,1)S(1)} %copy.7), channel_id=1, replica_groups={{64,72,80,88,96,104,112,120,0,8,16,24,32,40,48,56},{192,200,208,216,224..., dimensions={0} | all-to-all | bytes 32768 | tf_op jit(solution)/shard_map/all_to_all | solution.py:113
  34.8 0.1 slice_bitcast_fusion.1
  34.9 0.6 %pad_maximum_fusion.1 = bf16[2,64,64]{2,1,0:T(8,128)(2,1)} fusion(bf16[1,64,64]{2,1,0:T(8,128)(2,1)S(1)} %get-tuple-element.6, bf16[1,64,64]{2,1,0:T(8,128)(2,1)S(1)} %get-tuple-element.5), kind=kLoop, calls=%fused_computation.6 | loop fusion | flops 8192 | bytes 32768 | tf_op jit(solution)/shard_map/stack | solution.py:120
  (7 shorter events, 0.1 us)

commit v5 on v4

--- a/solution.py
+++ b/solution.py
@@ -36,9 +36,23 @@
     noise_copy = pltpu.make_async_copy(noise_hbm.at[0], noise, sem.at[1])
     vis_copy = pltpu.make_async_copy(vis_hbm.at[0, 0], vis, sem.at[2])
     cycle_copy = pltpu.make_async_copy(cycle_hbm.at[0], cycle, sem.at[3])
-    beam_copy = pltpu.make_async_copy(beam_hbm.at[0, 0], beam, sem.at[4])
-    for copy in (count_copy, noise_copy, vis_copy, cycle_copy, beam_copy):
+    lead_copy, rest_copy = (
+        pltpu.make_async_copy(beam_hbm.at[0, 0, pl.ds(s, 2)], beam.at[pl.ds(s, 2)], sem.at[4 + s // 2])
+        for s in (0, 2)
+    )
+    for copy in (count_copy, noise_copy, vis_copy, cycle_copy, lead_copy):
         copy.start()
+    count_copy.wait()
+    own_count = count[lax.axis_index("ma")]
+
+    @pl.when(own_count > 2)
+    def _():
+        rest_copy.start()
+
+    @pl.when(own_count <= 2)
+    def _():
+        beam[pl.ds(2, 2)] = jnp.zeros((2, 2, LT, NVIS), jnp.bfloat16)
+
 
     noise_copy.wait()
     column = jnp.broadcast_to(noise[...], (LT, NVIS)).T
@@ -47,17 +61,21 @@
         lanes = pl.ds(128 * k, 128)
         weighted[:, lanes] = (column * vis[:, lanes].astype(jnp.float32)).astype(jnp.bfloat16)
 
-    count_copy.wait()
-    own_count = count[lax.axis_index("ma")]
     cycle_copy.wait()
-    synth = jnp.concatenate(
-        [
-            jnp.where(s < own_count, cycle[s], jnp.zeros((RINGS, LT), jnp.bfloat16))
-            for s in range(SLOTS)
-        ],
-        axis=1,
-    )
-    beam_copy.wait()
+    used = []
+    for s in range(SLOTS):
+        acc[s] = jnp.where(s < own_count, cycle[s], jnp.zeros((RINGS, LT), jnp.bfloat16)).astype(
+            jnp.float32
+        )
+        rows = [acc[s, pl.ds(2 * d + p, n, stride=2), :] for p in range(2) for d, n in RUNS]
+        used.append(jnp.concatenate(rows).astype(jnp.bfloat16))
+    synth = jnp.concatenate(used, axis=1)
+    lead_copy.wait()
+
+    @pl.when(own_count > 2)
+    def _():
+        rest_copy.wait()
+
     for part in range(2):
         tiles = beam[:, part].reshape(SLOTS * LT, NVIS)
         gain[pl.ds(part * RINGS, RINGS)] = jnp.dot(
@@ -73,11 +91,8 @@
 
     low = lax.broadcasted_iota(jnp.int32, (CYCLES, 128), 1) < 64
     for k in range(SETS // 128):
-        acc[k] = total[:, 128 * k : 128 * (k + 1)]
-        even, odd = (
-            jnp.concatenate([acc[k, pl.ds(2 * d + p, n, stride=2), :] for d, n in RUNS])
-            for p in range(2)
-        )
+        lanes = slice(128 * k, 128 * (k + 1))
+        even, odd = total[:CYCLES, lanes], total[CYCLES:, lanes]
         low_band = jnp.where(low, even, pltpu.roll(odd, 64, 1)).astype(jnp.bfloat16)
         high_band = jnp.where(low, pltpu.roll(even, 64, 1), odd).astype(jnp.bfloat16)
         for i in range(XS):
@@ -99,9 +114,9 @@
             pltpu.VMEM((SLOTS, RINGS, LT), jnp.bfloat16),
             pltpu.VMEM((NVIS, SETS), jnp.bfloat16),
             pltpu.VMEM((2 * RINGS, NVIS), jnp.bfloat16),
-            pltpu.VMEM((SETS // 128, RINGS, 128), jnp.float32),
+            pltpu.VMEM((SLOTS, RINGS, LT), jnp.float32),
             pltpu.SMEM((CYCLES,), jnp.int32),
-            pltpu.SemaphoreType.DMA((5,)),
+            pltpu.SemaphoreType.DMA((6,)),
         ],
         compiler_params=pltpu.CompilerParams(vmem_limit_bytes=56 * 1024 * 1024),
     )(tile_count, visibility, noise_weight, transfer, legendre)

time: 35.9 us -> 35.7 us (level)
  blocking collectives: 32.6 us -> 32.1 us
    all_to_all x1, blocking collectives: 16.4 us -> 15.8 us  [local(): lax.all_to_all((band_sum * (1.0 / BANDS)).transpose(1, 0, 2), 'ma', 0, 0,...]
where the time goes in v5:
time: 35.7 us; the launch traced here: 35.3 us
  blocking collectives  32.1 us (90%)
  Pallas kernels  2.45 us (7%)
  other arithmetic  0.66 us (2%)
    all_to_all x1, blocking collectives, local(): lax.all_to_all(bands.reshape(XS * BANDS, ZS, 128), ('ma', 'freq'), 0, 0,...  16.2 us
    all_to_all x1, blocking collectives, local(): lax.all_to_all((band_sum * (1.0 / BANDS)).transpose(1, 0, 2), 'ma', 0, 0,...  15.8 us
    pallas_call x1, Pallas kernels, local(): pl.pallas_call(modes_kernel, out_shape=pltpu.VMEM((XS, BANDS, ZS, 128), j...  2.45 us

profile of v5, /device:TPU:1, one launch (start us, length us, event | category | flops | bytes accessed | tf_op | source)
XLA Modules:
  0.0 35.3 jit_solution(3980697469687605982)
XLA Ops:
  0.0 2.5 %shard_map.55 = bf16[4,8,16,128]{3,2,1,0:T(8,128)(2,1)S(1)} custom-call(s32[64]{0:T(128)} %count_hbm.1, bf16[1,1,512,512]{3,2,1,0:T(8,128)(2,1)} %vis_hbm.1, f32[1,1,512]{2,1,0:T(1,128)} %noise_hbm.1, bf16[1,1,4,2,128,512]{5,4,3,2,1,0:T(8,128)(2,1)} %beam_hbm.1, bf16[1,4,128,128]{3,2,1,0:T(8,128)(2,1)} %cycle_hbm.1), custom_call_target="tpu_custom_call" | custom-call | tf_op jit(solution)/shard_map/pallas_call | solution.py:105
  2.5 16.2 %all_to_all.10 = bf16[32,16,128]{2,1,0:T(8,128)(2,1)S(1)} all-to-all(bf16[32,16,128]{2,1,0:T(8,128)(2,1)S(1)} %bitcast.14), channel_id=1, replica_groups={{261,262,263,256,257,258,259,260,389,390,391,384,385,386,387,388,5,6,7,..., dimensions={0} | all-to-all | bytes 262144 | tf_op jit(solution)/shard_map/all_to_all | solution.py:123
  18.8 15.8 %all_to_all.11 = bf16[16,4,128]{2,1,0:T(4,128)(2,1)S(1)} all-to-all(bf16[16,4,128]{2,1,0:T(4,128)(2,1)S(1)} %copy.7), channel_id=1, replica_groups={{64,72,80,88,96,104,112,120,0,8,16,24,32,40,48,56},{192,200,208,216,224..., dimensions={0} | all-to-all | bytes 32768 | tf_op jit(solution)/shard_map/all_to_all | solution.py:128
  34.6 0.1 slice_bitcast_fusion.1
  34.7 0.6 %pad_maximum_fusion.1 = bf16[2,64,64]{2,1,0:T(8,128)(2,1)} fusion(bf16[1,64,64]{2,1,0:T(8,128)(2,1)S(1)} %get-tuple-element.6, bf16[1,64,64]{2,1,0:T(8,128)(2,1)S(1)} %get-tuple-element.5), kind=kLoop, calls=%fused_computation.6 | loop fusion | flops 8192 | bytes 32768 | tf_op jit(solution)/shard_map/stack | solution.py:135
  (7 shorter events, 0.1 us)

commit v6 on v5

--- a/solution.py
+++ b/solution.py
@@ -68,7 +68,7 @@
             jnp.float32
         )
         rows = [acc[s, pl.ds(2 * d + p, n, stride=2), :] for p in range(2) for d, n in RUNS]
-        used.append(jnp.concatenate(rows).astype(jnp.bfloat16))
+        used.append((jnp.concatenate(rows) * (1.0 / BANDS)).astype(jnp.bfloat16))
     synth = jnp.concatenate(used, axis=1)
     lead_copy.wait()
 
@@ -126,12 +126,11 @@
     )
     band_sum = jnp.sum(by_slab.reshape(XS, BANDS, ZS, 128).astype(jnp.float32), axis=1)
     by_line = lax.all_to_all(
-        (band_sum * (1.0 / BANDS)).transpose(1, 0, 2),
+        band_sum.transpose(1, 0, 2),
         "ma", 0, 0, tiled=True, axis_index_groups=LINE_GROUPS,
     )
-    modes = by_line.transpose(1, 0, 2)
-    modes = jnp.concatenate([modes[:, ZS - FIRST_Z :], modes[:, : ZS - FIRST_Z]], axis=1)
-    modes = jnp.concatenate([modes[XS - FIRST_X :], modes[: XS - FIRST_X]]).reshape(CYCLES, 128)
+    modes = by_line.reshape(2, ZS // 2, 2, XS // 2, 128).transpose(2, 3, 0, 1, 4)
+    modes = lax.rev(modes, (0, 2)).reshape(CYCLES, 128)
     return jnp.stack([modes[:, :64], modes[:, 64:]]).astype(jnp.bfloat16)
 
 

time: 35.7 us -> 35.7 us (level)
  no operation moved by 1% of the time
where the time goes in v6:
time: 35.7 us; the launch traced here: 35.3 us
  blocking collectives  32.1 us (90%)
  Pallas kernels  2.45 us (7%)
  other arithmetic  0.65 us (2%)
    all_to_all x1, blocking collectives, local(): lax.all_to_all(bands.reshape(XS * BANDS, ZS, 128), ('ma', 'freq'), 0, 0,...  16.2 us
    all_to_all x1, blocking collectives, local(): lax.all_to_all(band_sum.transpose(1, 0, 2), 'ma', 0, 0, tiled=True, axis_...  15.8 us
    pallas_call x1, Pallas kernels, local(): pl.pallas_call(modes_kernel, out_shape=pltpu.VMEM((XS, BANDS, ZS, 128), j...  2.45 us

profile of v6, /device:TPU:1, one launch (start us, length us, event | category | flops | bytes accessed | tf_op | source)
XLA Modules:
  0.0 35.3 jit_solution(9270414977272695998)
XLA Ops:
  0.0 2.5 %shard_map.55 = bf16[4,8,16,128]{3,2,1,0:T(8,128)(2,1)S(1)} custom-call(s32[64]{0:T(128)} %count_hbm.1, bf16[1,1,512,512]{3,2,1,0:T(8,128)(2,1)} %vis_hbm.1, f32[1,1,512]{2,1,0:T(1,128)} %noise_hbm.1, bf16[1,1,4,2,128,512]{5,4,3,2,1,0:T(8,128)(2,1)} %beam_hbm.1, bf16[1,4,128,128]{3,2,1,0:T(8,128)(2,1)} %cycle_hbm.1), custom_call_target="tpu_custom_call" | custom-call | tf_op jit(solution)/shard_map/pallas_call | solution.py:105
  2.5 16.2 %all_to_all.10 = bf16[32,16,128]{2,1,0:T(8,128)(2,1)S(1)} all-to-all(bf16[32,16,128]{2,1,0:T(8,128)(2,1)S(1)} %bitcast.13), channel_id=1, replica_groups={{261,262,263,256,257,258,259,260,389,390,391,384,385,386,387,388,5,6,7,..., dimensions={0} | all-to-all | bytes 262144 | tf_op jit(solution)/shard_map/all_to_all | solution.py:123
  18.7 15.8 %all_to_all.11 = bf16[16,4,128]{2,1,0:T(4,128)(2,1)S(1)} all-to-all(bf16[16,4,128]{2,1,0:T(4,128)(2,1)S(1)} %copy.7), channel_id=1, replica_groups={{64,72,80,88,96,104,112,120,0,8,16,24,32,40,48,56},{192,200,208,216,224..., dimensions={0} | all-to-all | bytes 32768 | tf_op jit(solution)/shard_map/all_to_all | solution.py:128
  34.6 0.1 slice_bitcast_fusion.1
  34.7 0.6 %pad_maximum_fusion = bf16[2,64,64]{2,1,0:T(8,128)(2,1)} fusion(bf16[1,64,64]{2,1,0:T(8,128)(2,1)S(1)} %get-tuple-element.6, bf16[1,64,64]{2,1,0:T(8,128)(2,1)S(1)} %get-tuple-element.5), kind=kLoop, calls=%fused_computation.1 | loop fusion | flops 8192 | bytes 32768 | tf_op jit(solution)/shard_map/stack | solution.py:134
  (4 shorter events, 0.0 us)

commit v7 on v6

--- a/solution.py
+++ b/solution.py
@@ -49,11 +49,6 @@
     def _():
         rest_copy.start()
 
-    @pl.when(own_count <= 2)
-    def _():
-        beam[pl.ds(2, 2)] = jnp.zeros((2, 2, LT, NVIS), jnp.bfloat16)
-
-
     noise_copy.wait()
     column = jnp.broadcast_to(noise[...], (LT, NVIS)).T
     vis_copy.wait()
@@ -71,16 +66,19 @@
         used.append((jnp.concatenate(rows) * (1.0 / BANDS)).astype(jnp.bfloat16))
     synth = jnp.concatenate(used, axis=1)
     lead_copy.wait()
+    for part in range(2):
+        gain[pl.ds(part * RINGS, RINGS)] = jnp.dot(
+            synth[:, : 2 * LT], beam[:2, part].reshape(2 * LT, NVIS), preferred_element_type=jnp.float32
+        ).astype(jnp.bfloat16)
 
     @pl.when(own_count > 2)
     def _():
         rest_copy.wait()
-
-    for part in range(2):
-        tiles = beam[:, part].reshape(SLOTS * LT, NVIS)
-        gain[pl.ds(part * RINGS, RINGS)] = jnp.dot(
-            synth, tiles, preferred_element_type=jnp.float32
-        ).astype(jnp.bfloat16)
+        for part in range(2):
+            tiles = beam[:, part].reshape(SLOTS * LT, NVIS)
+            gain[pl.ds(part * RINGS, RINGS)] = jnp.dot(
+                synth, tiles, preferred_element_type=jnp.float32
+            ).astype(jnp.bfloat16)
 
     rows = jnp.dot(gain[...], weighted[...], preferred_element_type=jnp.float32)
     real, imag = rows[:RINGS], rows[RINGS:]

time: 35.7 us -> 35.7 us (level)
  no operation moved by 1% of the time
where the time goes in v7:
time: 35.7 us; the launch traced here: 35.4 us
  blocking collectives  32 us (90%)
  Pallas kernels  2.55 us (7%)
  other arithmetic  0.65 us (2%)
    all_to_all x1, blocking collectives, local(): lax.all_to_all(bands.reshape(XS * BANDS, ZS, 128), ('ma', 'freq'), 0, 0,...  16.3 us
    all_to_all x1, blocking collectives, local(): lax.all_to_all(band_sum.transpose(1, 0, 2), 'ma', 0, 0, tiled=True, axis_...  15.8 us
    pallas_call x1, Pallas kernels, local(): pl.pallas_call(modes_kernel, out_shape=pltpu.VMEM((XS, BANDS, ZS, 128), j...  2.55 us

profile of v7, /device:TPU:1, one launch (start us, length us, event | category | flops | bytes accessed | tf_op | source)
XLA Modules:
  0.0 35.4 jit_solution(11926540805002226342)
XLA Ops:
  0.0 2.5 %shard_map.55 = bf16[4,8,16,128]{3,2,1,0:T(8,128)(2,1)S(1)} custom-call(s32[64]{0:T(128)} %count_hbm.1, bf16[1,1,512,512]{3,2,1,0:T(8,128)(2,1)} %vis_hbm.1, f32[1,1,512]{2,1,0:T(1,128)} %noise_hbm.1, bf16[1,1,4,2,128,512]{5,4,3,2,1,0:T(8,128)(2,1)} %beam_hbm.1, bf16[1,4,128,128]{3,2,1,0:T(8,128)(2,1)} %cycle_hbm.1), custom_call_target="tpu_custom_call" | custom-call | tf_op jit(solution)/shard_map/pallas_call | solution.py:103
  2.6 16.3 %all_to_all.10 = bf16[32,16,128]{2,1,0:T(8,128)(2,1)S(1)} all-to-all(bf16[32,16,128]{2,1,0:T(8,128)(2,1)S(1)} %bitcast.13), channel_id=1, replica_groups={{261,262,263,256,257,258,259,260,389,390,391,384,385,386,387,388,5,6,7,..., dimensions={0} | all-to-all | bytes 262144 | tf_op jit(solution)/shard_map/all_to_all | solution.py:121
  18.9 15.8 %all_to_all.11 = bf16[16,4,128]{2,1,0:T(4,128)(2,1)S(1)} all-to-all(bf16[16,4,128]{2,1,0:T(4,128)(2,1)S(1)} %copy.7), channel_id=1, replica_groups={{64,72,80,88,96,104,112,120,0,8,16,24,32,40,48,56},{192,200,208,216,224..., dimensions={0} | all-to-all | bytes 32768 | tf_op jit(solution)/shard_map/all_to_all | solution.py:126
  34.7 0.1 slice_bitcast_fusion.1
  34.7 0.6 %pad_maximum_fusion = bf16[2,64,64]{2,1,0:T(8,128)(2,1)} fusion(bf16[1,64,64]{2,1,0:T(8,128)(2,1)S(1)} %get-tuple-element.6, bf16[1,64,64]{2,1,0:T(8,128)(2,1)S(1)} %get-tuple-element.5), kind=kLoop, calls=%fused_computation.1 | loop fusion | flops 8192 | bytes 32768 | tf_op jit(solution)/shard_map/stack | solution.py:132
  (4 shorter events, 0.0 us)

commit v8 on v7

--- a/solution.py
+++ b/solution.py
@@ -40,7 +40,7 @@
         pltpu.make_async_copy(beam_hbm.at[0, 0, pl.ds(s, 2)], beam.at[pl.ds(s, 2)], sem.at[4 + s // 2])
         for s in (0, 2)
     )
-    for copy in (count_copy, noise_copy, vis_copy, cycle_copy, lead_copy):
+    for copy in (count_copy, noise_copy, cycle_copy, lead_copy, vis_copy):
         copy.start()
     count_copy.wait()
     own_count = count[lax.axis_index("ma")]
@@ -51,11 +51,6 @@
 
     noise_copy.wait()
     column = jnp.broadcast_to(noise[...], (LT, NVIS)).T
-    vis_copy.wait()
-    for k in range(SETS // 128):
-        lanes = pl.ds(128 * k, 128)
-        weighted[:, lanes] = (column * vis[:, lanes].astype(jnp.float32)).astype(jnp.bfloat16)
-
     cycle_copy.wait()
     used = []
     for s in range(SLOTS):
@@ -70,6 +65,11 @@
         gain[pl.ds(part * RINGS, RINGS)] = jnp.dot(
             synth[:, : 2 * LT], beam[:2, part].reshape(2 * LT, NVIS), preferred_element_type=jnp.float32
         ).astype(jnp.bfloat16)
+
+    vis_copy.wait()
+    for k in range(SETS // 128):
+        lanes = pl.ds(128 * k, 128)
+        weighted[:, lanes] = (column * vis[:, lanes].astype(jnp.float32)).astype(jnp.bfloat16)
 
     @pl.when(own_count > 2)
     def _():

time: 35.7 us -> 35.7 us (level)
  no operation moved by 1% of the time
where the time goes in v8:
time: 35.7 us; the launch traced here: 35.3 us
  blocking collectives  32 us (90%)
  Pallas kernels  2.55 us (7%)
  other arithmetic  0.65 us (2%)
    all_to_all x1, blocking collectives, local(): lax.all_to_all(bands.reshape(XS * BANDS, ZS, 128), ('ma', 'freq'), 0, 0,...  16.3 us
    all_to_all x1, blocking collectives, local(): lax.all_to_all(band_sum.transpose(1, 0, 2), 'ma', 0, 0, tiled=True, axis_...  15.8 us
    pallas_call x1, Pallas kernels, local(): pl.pallas_call(modes_kernel, out_shape=pltpu.VMEM((XS, BANDS, ZS, 128), j...  2.55 us

profile of v8, /device:TPU:1, one launch (start us, length us, event | category | flops | bytes accessed | tf_op | source)
XLA Modules:
  0.0 35.3 jit_solution(7989286201041144037)
XLA Ops:
  0.0 2.5 %shard_map.55 = bf16[4,8,16,128]{3,2,1,0:T(8,128)(2,1)S(1)} custom-call(s32[64]{0:T(128)} %count_hbm.1, bf16[1,1,512,512]{3,2,1,0:T(8,128)(2,1)} %vis_hbm.1, f32[1,1,512]{2,1,0:T(1,128)} %noise_hbm.1, bf16[1,1,4,2,128,512]{5,4,3,2,1,0:T(8,128)(2,1)} %beam_hbm.1, bf16[1,4,128,128]{3,2,1,0:T(8,128)(2,1)} %cycle_hbm.1), custom_call_target="tpu_custom_call" | custom-call | tf_op jit(solution)/shard_map/pallas_call | solution.py:103
  2.6 16.3 %all_to_all.10 = bf16[32,16,128]{2,1,0:T(8,128)(2,1)S(1)} all-to-all(bf16[32,16,128]{2,1,0:T(8,128)(2,1)S(1)} %bitcast.13), channel_id=1, replica_groups={{261,262,263,256,257,258,259,260,389,390,391,384,385,386,387,388,5,6,7,..., dimensions={0} | all-to-all | bytes 262144 | tf_op jit(solution)/shard_map/all_to_all | solution.py:121
  18.9 15.8 %all_to_all.11 = bf16[16,4,128]{2,1,0:T(4,128)(2,1)S(1)} all-to-all(bf16[16,4,128]{2,1,0:T(4,128)(2,1)S(1)} %copy.7), channel_id=1, replica_groups={{64,72,80,88,96,104,112,120,0,8,16,24,32,40,48,56},{192,200,208,216,224..., dimensions={0} | all-to-all | bytes 32768 | tf_op jit(solution)/shard_map/all_to_all | solution.py:126
  34.6 0.1 slice_bitcast_fusion.1
  34.7 0.6 %pad_maximum_fusion = bf16[2,64,64]{2,1,0:T(8,128)(2,1)} fusion(bf16[1,64,64]{2,1,0:T(8,128)(2,1)S(1)} %get-tuple-element.6, bf16[1,64,64]{2,1,0:T(8,128)(2,1)S(1)} %get-tuple-element.5), kind=kLoop, calls=%fused_computation.1 | loop fusion | flops 8192 | bytes 32768 | tf_op jit(solution)/shard_map/stack | solution.py:132
  (4 shorter events, 0.0 us)
